TPU v7x, 32 devices: a whole 2x2x4 slice. The times are simulated.
32 devices in a mesh: prow: 8 (over y, x, core), pcol: 4 (over z).
Axes of the slice: x: 2, y: 2, z: 4, core: 2. Of those that a mesh axis runs over, the one named last changes fastest.
Arguments:
- right_side: bfloat16 [5, 32, 128, 256], P(None, ('prow', 'pcol')), may hold values from -6 to 6
- lower_inverse: bfloat16 [5, 32, 128, 128], P(None, ('prow', 'pcol')), may hold values from -1.5 to 1.5
- upper_inverse: bfloat16 [5, 32, 128, 128], P(None, ('prow', 'pcol')), may hold values from -1.5 to 1.5
- lower_blocks: bfloat16 [4, 32, 24, 128, 128], P(None, 'prow', 'pcol'), may hold values from -0.078125 to 0.078125
- lower_index: int32 [4, 32, 24], P(None, 'prow', 'pcol'), may hold values from 0 to 31, as said below
- upper_blocks: bfloat16 [4, 32, 24, 128, 128], P(None, 'prow', 'pcol'), may hold values from -0.078125 to 0.078125
- upper_index: int32 [4, 32, 24], P(None, 'prow', 'pcol'), may hold values from 8 to 39, as said below
Outputs:
- solution: bfloat16 [5, 32, 128, 256], P(None, ('prow', 'pcol'))
Inputs may be any that keep to these rules, and one draw needn't show every extreme that they name: lower_index[l, m, j] names a supernode of a level below l + 1; numbers may repeat. upper_index[l, m, j] names a supernode of a level above l; numbers may repeat.
All inputs are finite; a program needn't handle non-finite values.
Results may differ from a plain program's by a relative error of at most 0.014.
Values may be sent and summed in bfloat16 or wider, within the bound.
A program may use at most 128 MiB of HBM per device.

v0:
```python
import jax
import jax.numpy as jnp
from jax import lax
from jax.sharding import PartitionSpec as P


def block_terms(blocks, pointers, stored):
    picked = jnp.take(stored, pointers, axis=0)
    return jnp.einsum("mkvw,mkwn->mvn", blocks, picked, preferred_element_type=jnp.float32)


def spread(solved):
    return lax.all_gather(solved, "prow", axis=0, tiled=True)


def apply_inverse(inverse, remain):
    product = jnp.einsum("uvw,uwn->uvn", inverse, remain, preferred_element_type=jnp.float32)
    return product.astype(jnp.bfloat16)


def solve_levels(
    first_inverse, inverses, blocks, pointers, sources, order, offset, per_group, levels
):
    breadth = sources[0].shape[1]
    columns = sources[0].shape[2]
    stored = jnp.zeros((levels * per_group, breadth, columns), jnp.bfloat16)
    solved = {order[0] - offset: apply_inverse(first_inverse, sources[order[0] - offset])}
    for turn in range(1, len(order)):
        height = order[turn]
        before = order[turn - 1]
        stored = lax.dynamic_update_slice_in_dim(
            stored, spread(solved[before]), before * per_group, 0
        )
        row_set = min(height, before)
        partial_value = block_terms(blocks[row_set], pointers[row_set], stored)
        totals = lax.psum_scatter(partial_value, "pcol", scatter_dimension=0, tiled=True)
        remain = (sources[height].astype(jnp.float32) - totals).astype(jnp.bfloat16)
        solved[height] = apply_inverse(inverses[height], remain)
    return solved


def shards(
    right_side, lower_inverse, upper_inverse, lower_blocks, lower_index, upper_blocks, upper_index
):
    levels = right_side.shape[0]
    per_group = lax.axis_size("prow") * right_side.shape[1]
    sources = [right_side[height] for height in range(levels)]
    forward = solve_levels(
        lower_inverse[0],
        lower_inverse,
        lower_blocks,
        lower_index,
        sources,
        list(range(levels)),
        0,
        per_group,
        levels,
    )
    lower_list = [forward[height] for height in range(levels)]
    order = list(range(levels - 1, -1, -1))
    backward = solve_levels(
        upper_inverse[levels - 1],
        upper_inverse,
        upper_blocks,
        upper_index,
        lower_list,
        order,
        0,
        per_group,
        levels,
    )
    return jnp.stack([backward[height] for height in range(levels)])


def solution(mesh):
    placed = (
        P(None, ("prow", "pcol"), None, None),
        P(None, ("prow", "pcol"), None, None),
        P(None, ("prow", "pcol"), None, None),
        P(None, "prow", "pcol", None, None),
        P(None, "prow", "pcol"),
        P(None, "prow", "pcol", None, None),
        P(None, "prow", "pcol"),
    )
    return jax.shard_map(
        shards,
        mesh=mesh,
        in_specs=placed,
        out_specs=P(None, ("prow", "pcol"), None, None),
        check_vma=False,
    )
```

profile of v0, /device:TPU:0, one launch (start us, length us, event | category | flops | bytes accessed | tf_op | source)
XLA Modules:
  0.0 337.5 jit_solution(11396718225179977087)
XLA Ops:
  6.5 1.4 compare_select_fusion
  7.9 1.4 compare_and_fusion
  10.5 11.3 %all-gather = bf16[1024,256]{1,0:T(8,128)(2,1)S(1)} all-gather(bf16[128,256]{1,0:T(8,128)(2,1)S(1)} %convolution_convert_fusion.9), channel_id=2, replica_groups=mesh['prow'=8,'pcol'=4] {'prow'}, dimensions={0}, use_global_device_ids=true | all-gather | bytes 589824 | tf_op jit(solution)/shard_map/all_gather | solution.py:13
  22.1 1.8 gather_fusion
  23.9 2.6 copy.27
  26.5 3.1 fusion.24
  29.9 21.8 %reduce-scatter.9.cloned.1.call-done = f32[1,128,256]{1,2,0:T(8,128)} async-done(((f32[4,128,256]{1,2,0:T(8,128)}), f32[1,128,256]{1,2,0:T(8,128)}) %reduce-scatter.9.cloned.1.call-update) | async-done | bytes 131088 | tf_op jit(solution)/shard_map/reduce_scatter | solution.py:36
  52.8 11.0 %all-gather.1 = bf16[1024,256]{0,1:T(8,128)(2,1)} all-gather(bf16[128,256]{0,1:T(8,128)(2,1)S(1)} %bitcast.267), channel_id=3, replica_groups=mesh['prow'=8,'pcol'=4] {'prow'}, dimensions={0}, use_global_device_ids=true | all-gather | bytes 589824 | tf_op jit(solution)/shard_map/all_gather | solution.py:13
  63.8 1.2 copy.54
  65.1 1.8 gather_fusion.1
  66.9 2.6 copy.30
  69.6 3.0 fusion.27
  72.9 19.0 %reduce-scatter.11.cloned.1.call-done = f32[1,128,256]{1,2,0:T(8,128)} async-done(((f32[4,128,256]{1,2,0:T(8,128)}), f32[1,128,256]{1,2,0:T(8,128)}) %reduce-scatter.11.cloned.1.call-update) | async-done | bytes 131088 | tf_op jit(solution)/shard_map/reduce_scatter | solution.py:36
  92.9 11.0 %all-gather.2 = bf16[1024,256]{0,1:T(8,128)(2,1)} all-gather(bf16[128,256]{0,1:T(8,128)(2,1)S(1)} %bitcast.268), channel_id=4, replica_groups=mesh['prow'=8,'pcol'=4] {'prow'}, dimensions={0}, use_global_device_ids=true | all-gather | bytes 589824 | tf_op jit(solution)/shard_map/all_gather | solution.py:13
  103.9 1.2 copy.55
  105.2 1.8 gather_fusion.2
  107.0 2.6 copy.33
  109.7 3.0 fusion.30
  113.0 19.0 %reduce-scatter.13.cloned.1.call-done = f32[1,128,256]{1,2,0:T(8,128)} async-done(((f32[4,128,256]{1,2,0:T(8,128)}), f32[1,128,256]{1,2,0:T(8,128)}) %reduce-scatter.13.cloned.1.call-update) | async-done | bytes 131088 | tf_op jit(solution)/shard_map/reduce_scatter | solution.py:36
  133.0 10.9 %all-gather.3 = bf16[1024,256]{0,1:T(8,128)(2,1)} all-gather(bf16[128,256]{0,1:T(8,128)(2,1)S(1)} %bitcast.269), channel_id=5, replica_groups=mesh['prow'=8,'pcol'=4] {'prow'}, dimensions={0}, use_global_device_ids=true | all-gather | bytes 589824 | tf_op jit(solution)/shard_map/all_gather | solution.py:13
  143.9 1.2 copy.56
  145.2 1.9 gather_fusion.3
  147.1 1.9 copy.35
  149.1 2.5 fusion.33
  151.9 19.0 %reduce-scatter.15.cloned.1.call-done = f32[1,128,256]{1,2,0:T(8,128)} async-done(((f32[4,128,256]{1,2,0:T(8,128)}), f32[1,128,256]{1,2,0:T(8,128)}) %reduce-scatter.15.cloned.1.call-update) | async-done | bytes 131088 | tf_op jit(solution)/shard_map/reduce_scatter | solution.py:36
  172.1 9.9 %all-gather.4 = bf16[1024,256]{0,1:T(8,128)(2,1)S(1)} all-gather(bf16[128,256]{0,1:T(8,128)(2,1)S(1)} %bitcast.263), channel_id=6, replica_groups=mesh['prow'=8,'pcol'=4] {'prow'}, dimensions={0}, use_global_device_ids=true | all-gather | bytes 589824 | tf_op jit(solution)/shard_map/all_gather | solution.py:13
  182.5 1.8 gather_fusion.4
  184.3 2.6 copy.37
  187.0 3.0 fusion.36
  190.2 19.1 %reduce-scatter.17.cloned.1.call-done = f32[1,128,256]{1,2,0:T(8,128)} async-done(((f32[4,128,256]{1,2,0:T(8,128)}), f32[1,128,256]{1,2,0:T(8,128)}) %reduce-scatter.17.cloned.1.call-update) | async-done | bytes 131088 | tf_op jit(solution)/shard_map/reduce_scatter | solution.py:36
  210.3 11.0 %all-gather.5 = bf16[1024,256]{0,1:T(8,128)(2,1)} all-gather(bf16[128,256]{0,1:T(8,128)(2,1)S(1)} %bitcast.264), channel_id=7, replica_groups=mesh['prow'=8,'pcol'=4] {'prow'}, dimensions={0}, use_global_device_ids=true | all-gather | bytes 589824 | tf_op jit(solution)/shard_map/all_gather | solution.py:13
  221.3 1.2 copy.58
  222.6 1.8 gather_fusion.5
  224.5 2.6 copy.39
  227.1 3.0 fusion.39
  230.3 19.1 %reduce-scatter.19.cloned.1.call-done = f32[1,128,256]{1,2,0:T(8,128)} async-done(((f32[4,128,256]{1,2,0:T(8,128)}), f32[1,128,256]{1,2,0:T(8,128)}) %reduce-scatter.19.cloned.1.call-update) | async-done | bytes 131088 | tf_op jit(solution)/shard_map/reduce_scatter | solution.py:36
  250.4 11.0 %all-gather.6 = bf16[1024,256]{0,1:T(8,128)(2,1)} all-gather(bf16[128,256]{0,1:T(8,128)(2,1)S(1)} %bitcast.265), channel_id=8, replica_groups=mesh['prow'=8,'pcol'=4] {'prow'}, dimensions={0}, use_global_device_ids=true | all-gather | bytes 589824 | tf_op jit(solution)/shard_map/all_gather | solution.py:13
  261.4 1.2 copy.59
  262.7 1.8 gather_fusion.6
  264.6 2.6 copy.41
  267.2 3.0 fusion.42
  270.4 19.1 %reduce-scatter.21.cloned.1.call-done = f32[1,128,256]{1,2,0:T(8,128)} async-done(((f32[4,128,256]{1,2,0:T(8,128)}), f32[1,128,256]{1,2,0:T(8,128)}) %reduce-scatter.21.cloned.1.call-update) | async-done | bytes 131088 | tf_op jit(solution)/shard_map/reduce_scatter | solution.py:36
  290.6 11.0 %all-gather.7 = bf16[1024,256]{0,1:T(8,128)(2,1)} all-gather(bf16[128,256]{0,1:T(8,128)(2,1)S(1)} %bitcast.266), channel_id=9, replica_groups=mesh['prow'=8,'pcol'=4] {'prow'}, dimensions={0}, use_global_device_ids=true | all-gather | bytes 589824 | tf_op jit(solution)/shard_map/all_gather | solution.py:13
  301.5 1.2 copy.60
  302.8 1.9 gather_fusion.7
  304.7 1.9 copy.43
  306.6 2.6 fusion.45
  309.3 19.2 %reduce-scatter.23.cloned.1.call-done = f32[1,128,256]{2,1,0:T(8,128)} async-done(((f32[4,128,256]{2,1,0:T(8,128)}), f32[1,128,256]{2,1,0:T(8,128)}) %reduce-scatter.23.cloned.1.call-update) | async-done | bytes 131088 | tf_op jit(solution)/shard_map/reduce_scatter | solution.py:36
  (82 shorter events, 13.3 us)
Async XLA Ops:
  6.5 45.2 %reduce-scatter.9.cloned.1.call-start = ((), (), s32[]{:S(2)}) async-start(), calls=%async_computation.8 | async-start | bytes 655360 | tf_op jit(solution)/shard_map/reduce_scatter | solution.py:36
  26.5 3.1 copy-start
  29.6 62.2 %reduce-scatter.11.cloned.1.call-start = ((), (), s32[]{:S(2)}) async-start(), calls=%async_computation.9 | async-start | bytes 655360 | tf_op jit(solution)/shard_map/reduce_scatter | solution.py:36
  66.9 2.6 copy-start.10
  69.5 3.2 copy-start.3
  72.6 59.3 %reduce-scatter.13.cloned.1.call-start = ((), (), s32[]{:S(2)}) async-start(), calls=%async_computation.10 | async-start | bytes 655360 | tf_op jit(solution)/shard_map/reduce_scatter | solution.py:36
  107.0 2.6 copy-start.9
  109.7 3.2 copy-start.2
  112.7 58.1 %reduce-scatter.15.cloned.1.call-start = ((), (), s32[]{:S(2)}) async-start(), calls=%async_computation.11 | async-start | bytes 655360 | tf_op jit(solution)/shard_map/reduce_scatter | solution.py:36
  147.1 1.9 copy-start.8
  149.0 2.7 copy-start.1
  151.6 57.7 %reduce-scatter.17.cloned.1.call-start = ((), (), s32[]{:S(2)}) async-start(), calls=%async_computation.12 | async-start | bytes 655360 | tf_op jit(solution)/shard_map/reduce_scatter | solution.py:36
  184.3 2.6 copy-start.7
  190.0 59.4 %reduce-scatter.19.cloned.1.call-start = ((), (), s32[]{:S(2)}) async-start(), calls=%async_computation.13 | async-start | bytes 655360 | tf_op jit(solution)/shard_map/reduce_scatter | solution.py:36
  224.5 2.6 copy-start.6
  230.1 59.3 %reduce-scatter.21.cloned.1.call-start = ((), (), s32[]{:S(2)}) async-start(), calls=%async_computation.14 | async-start | bytes 655360 | tf_op jit(solution)/shard_map/reduce_scatter | solution.py:36
  264.6 2.6 copy-start.5
  270.2 58.3 %reduce-scatter.23.cloned.1.call-start = ((), (), s32[]{:S(2)}) async-start(), calls=%async_computation.15 | async-start | bytes 655360 | tf_op jit(solution)/shard_map/reduce_scatter | solution.py:36
  304.7 1.9 copy-start.4
Sparse Core Ops, SparseCore 0:
  29.7 21.9 reduce-scatter.8
  72.7 19.0 reduce-scatter.10
  112.8 19.0 reduce-scatter.12
  151.7 19.0 reduce-scatter.14
  190.1 19.0 reduce-scatter.16
  230.3 19.0 reduce-scatter.18
  270.4 19.0 reduce-scatter.20
  309.4 19.0 reduce-scatter.22
where the time goes:
time: 339 us; the launch traced here: 337 us
  waiting for transfers between devices  155 us (46%)
  blocking collectives  87.2 us (26%)
  local copies, waits for them, and re-layouts  44.9 us (13%)
  matrix products  33.1 us (10%)
  between operations  13.8 us (4%)
    reduce_scatter x8, waiting for transfers between devices, solve_levels(): lax.psum_scatter(partial_value, 'pcol', scatter_dimension=0, tiled=True)  155 us
    all_gather x8, blocking collectives, spread(): return lax.all_gather(solved, 'prow', axis=0, tiled=True)  87.2 us
    gather x16, local copies, waits for them, and re-layouts, block_terms(): picked = jnp.take(stored, pointers, axis=0)  34.3 us
    dot_general x8, matrix products, block_terms(): jnp.einsum('mkvw,mkwn->mvn', blocks, picked, preferred_element_type=jnp.f...  23.4 us
    dot_general x9, matrix products, apply_inverse(): jnp.einsum('uvw,uwn->uvn', inverse, remain, preferred_element_type=jnp.fl...  9.72 us
    all_gather x7, local copies, waits for them, and re-layouts, spread(): return lax.all_gather(solved, 'prow', axis=0, tiled=True)  7.66 us
  transfers between devices with their start and end apart: 8, of which 8 were waited for; matrix products, arithmetic and copies ran while one was open for 0% of the time, Pallas kernels for 0%

commit v1 on v0

v1 whole, which is shorter than its diff:
```python
import functools

import jax
import jax.numpy as jnp
from jax import lax
from jax.experimental import pallas as pl
from jax.experimental.pallas import tpu as pltpu
from jax.sharding import PartitionSpec as P

MESH = pl.DeviceIdType.MESH
HALVES = 2


def flip(index, bits):
    bit = 1
    while bit <= bits:
        if bits & bit:
            index = index + bit - 2 * bit * lax.rem(lax.div(index, bit), 2)
        bit *= 2
    return index


def kernel(
    n_row, n_col, levels, nnz,
    rhs, linv, uinv, lblk, ublk, lidx, uidx, out,
    blk, land, cache, psend, precv, own, fsol,
    blk_sem, gather_send, gather_recv, relay_send, part_send, part_recv,
):
    climbs = levels - 1
    turns = 2 * climbs
    width = land.shape[-1]
    row = lax.axis_index("prow")
    col = lax.axis_index("pcol")
    core = lax.rem(row, 2)
    sibling = flip(row, 1)
    planes = [flip(row, 2 * j) for j in range(1, n_row // 2)]
    ends = [flip(col, j) for j in range(n_col - 1, 0, -1)]

    def block_copy(turn):
        source = lblk.at[turn] if turn < climbs else ublk.at[turns - 1 - turn]
        return pltpu.make_async_copy(source, blk.at[turn], blk_sem.at[turn])

    for turn in range(turns):
        block_copy(turn).start()

    barrier = pltpu.get_barrier_semaphore()
    for peer in planes + [sibling]:
        pl.semaphore_signal(barrier, inc=1, device_id=(peer, col), device_id_type=MESH)
    for peer in ends:
        pl.semaphore_signal(barrier, inc=1, device_id=(row, peer), device_id_type=MESH)

    def gather_copy(turn, half, peer):
        return pltpu.make_async_remote_copy(
            src_ref=land.at[turn, half, row],
            dst_ref=land.at[turn, half, row],
            send_sem=gather_send.at[turn, half, peer],
            recv_sem=gather_recv.at[turn, half, row],
            device_id=(peer, col),
            device_id_type=MESH,
        )

    def gather_arrival(turn, half, slot):
        return pltpu.make_async_remote_copy(
            src_ref=land.at[turn, half, slot],
            dst_ref=land.at[turn, half, slot],
            send_sem=gather_send.at[turn, half, slot],
            recv_sem=gather_recv.at[turn, half, slot],
            device_id=(sibling, col),
            device_id_type=MESH,
        )

    def relay_copy(turn, half, slot):
        return pltpu.make_async_remote_copy(
            src_ref=land.at[turn, half, slot],
            dst_ref=land.at[turn, half, slot],
            send_sem=relay_send.at[turn, half, lax.div(slot, 2)],
            recv_sem=gather_recv.at[turn, half, slot],
            device_id=(sibling, col),
            device_id_type=MESH,
        )

    def part_copy(turn, half, peer):
        return pltpu.make_async_remote_copy(
            src_ref=psend.at[turn, half, peer],
            dst_ref=precv.at[turn, half, col],
            send_sem=part_send.at[turn, half, peer],
            recv_sem=part_recv.at[turn, half, col],
            device_id=(row, peer),
            device_id_type=MESH,
        )

    def part_arrival(turn, half, peer):
        return pltpu.make_async_remote_copy(
            src_ref=psend.at[turn, half, peer],
            dst_ref=precv.at[turn, half, peer],
            send_sem=part_send.at[turn, half, peer],
            recv_sem=part_recv.at[turn, half, peer],
            device_id=(row, peer),
            device_id_type=MESH,
        )

    def columns(half):
        return slice(half * width, (half + 1) * width)

    def apply_inverse(inverse, remain):
        return jnp.dot(inverse, remain, preferred_element_type=jnp.float32).astype(jnp.bfloat16)

    def start_gather(turn, half, level, solved):
        land[turn, half, row] = solved
        for peer in planes:
            gather_copy(turn, half, peer).start()
        gather_copy(turn, half, sibling).start()
        cache[half, level * n_row + row] = solved

    def finish_gather(turn, half, level):
        for peer in planes:
            gather_arrival(turn, half, peer).wait_recv()
            relay_copy(turn, half, peer).start()
            cache[half, level * n_row + peer] = land[turn, half, peer]
        for slot in [sibling] + [flip(peer, 1) for peer in planes]:
            gather_arrival(turn, half, slot).wait_recv()
            cache[half, level * n_row + slot] = land[turn, half, slot]

    def finish_gather_sends(turn, half):
        for peer in planes + [sibling]:
            gather_copy(turn, half, peer).wait_send()
        for peer in planes:
            relay_copy(turn, half, peer).wait_send()

    def row_sum(turn, half, index, level, peer):
        left = jnp.concatenate([blk[turn, peer, k] for k in range(nnz)], axis=1)
        right = jnp.concatenate(
            [cache[half, index[level, peer, k]] for k in range(nnz)], axis=0
        )
        return jnp.dot(left, right, preferred_element_type=jnp.float32)

    def send_parts(turn, half, index, level):
        for peer in ends:
            psend[turn, half, peer] = row_sum(turn, half, index, level, peer).astype(jnp.bfloat16)
            part_copy(turn, half, peer).start()
        own[half] = row_sum(turn, half, index, level, col)

    def take_parts(turn, half):
        total = own[half]
        for peer in ends[::-1]:
            part_arrival(turn, half, peer).wait_recv()
            total = total + precv[turn, half, peer].astype(jnp.float32)
        return total

    def finish_part_sends(turn, half):
        for peer in ends:
            part_copy(turn, half, peer).wait_send()

    def step(turn, forward, last):
        before = turn if forward else turns - turn
        height = turn + 1 if forward else turns - 1 - turn
        index, level = (lidx, turn) if forward else (uidx, height)
        pltpu.make_async_copy(lblk.at[0], blk.at[turn], blk_sem.at[turn]).wait()
        for half in range(HALVES):
            finish_gather(turn, half, before)
            send_parts(turn, half, index, level)
        for half in range(HALVES):
            finish_gather_sends(turn, half)
            total = take_parts(turn, half)
            source = rhs[height, 0, :, columns(half)] if forward else fsol[height, half]
            remain = (source.astype(jnp.float32) - total).astype(jnp.bfloat16)
            if forward:
                solved = apply_inverse(linv[height, 0], remain)
                if last:
                    solved = apply_inverse(uinv[height, 0], solved)
                    out[height, 0, :, columns(half)] = solved
                else:
                    fsol[height, half] = solved
            else:
                solved = apply_inverse(uinv[height, 0], remain)
                out[height, 0, :, columns(half)] = solved
            if forward or not last:
                start_gather(turn + 1, half, height, solved)
            finish_part_sends(turn, half)

    first = []
    for half in range(HALVES):
        solved = apply_inverse(linv[0, 0], rhs[0, 0, :, columns(half)])
        fsol[0, half] = solved
        first.append(solved)
    pl.semaphore_wait(barrier, len(planes) + 1 + len(ends))
    for half in range(HALVES):
        start_gather(0, half, 0, first[half])

    lax.fori_loop(0, climbs - 1, lambda turn, _: step(turn, True, False), None)
    step(climbs - 1, True, True)
    lax.fori_loop(climbs, turns - 1, lambda turn, _: step(turn, False, False), None)
    step(turns - 1, False, True)


def shards(
    right_side, lower_inverse, upper_inverse, lower_blocks, lower_index, upper_blocks, upper_index
):
    n_row, n_col = lax.axis_size("prow"), lax.axis_size("pcol")
    levels, _, breadth, columns = right_side.shape
    climbs, rows, nnz = lower_index.shape
    turns = 2 * climbs
    width = columns // HALVES
    bf16 = jnp.bfloat16
    vmem = pl.BlockSpec(memory_space=pltpu.VMEM)
    smem = pl.BlockSpec(memory_space=pltpu.SMEM)
    hbm = pl.BlockSpec(memory_space=pl.ANY)
    dma = pltpu.SemaphoreType.DMA
    return pl.pallas_call(
        functools.partial(kernel, n_row, n_col, levels, nnz),
        out_shape=jax.ShapeDtypeStruct(right_side.shape, bf16),
        in_specs=[vmem, vmem, vmem, hbm, hbm, smem, smem],
        out_specs=vmem,
        scratch_shapes=[
            pltpu.VMEM((turns, rows, nnz, breadth, breadth), bf16),
            pltpu.VMEM((turns, HALVES, n_row, breadth, width), bf16),
            pltpu.VMEM((HALVES, levels * n_row, breadth, width), bf16),
            pltpu.VMEM((turns, HALVES, n_col, breadth, width), bf16),
            pltpu.VMEM((turns, HALVES, n_col, breadth, width), bf16),
            pltpu.VMEM((HALVES, breadth, width), jnp.float32),
            pltpu.VMEM((levels, HALVES, breadth, width), bf16),
            dma((turns,)),
            dma((turns, HALVES, n_row)),
            dma((turns, HALVES, n_row)),
            dma((turns, HALVES, n_row // 2)),
            dma((turns, HALVES, n_col)),
            dma((turns, HALVES, n_col)),
        ],
        compiler_params=pltpu.CompilerParams(
            collective_id=0, has_side_effects=True, vmem_limit_bytes=58 * 1024 * 1024
        ),
        cost_estimate=pl.CostEstimate(
            flops=2 * turns * rows * nnz * breadth * breadth * columns,
            bytes_accessed=2 * turns * rows * nnz * breadth * breadth,
            transcendentals=0,
        ),
    )(
        right_side, lower_inverse, upper_inverse,
        lower_blocks, upper_blocks, lower_index, upper_index,
    )


def solution(mesh):
    placed = (
        P(None, ("prow", "pcol"), None, None),
        P(None, ("prow", "pcol"), None, None),
        P(None, ("prow", "pcol"), None, None),
        P(None, "prow", "pcol", None, None),
        P(None, "prow", "pcol"),
        P(None, "prow", "pcol", None, None),
        P(None, "prow", "pcol"),
    )
    return jax.shard_map(
        shards,
        mesh=mesh,
        in_specs=placed,
        out_specs=P(None, ("prow", "pcol"), None, None),
        check_vma=False,
    )
```

time: 339 us -> 94.3 us (0.28)
  waiting for transfers between devices: 155 us -> 0 us
  Pallas kernels: 0 us -> 92.4 us
  blocking collectives: 87.2 us -> 0 us
  local copies, waits for them, and re-layouts: 44.9 us -> 1.72 us
  matrix products: 33.1 us -> 0 us
  between operations: 13.8 us -> 0.01 us
    reduce_scatter x8 -> x0, waiting for transfers between devices: 155 us -> none  [solve_levels(): lax.psum_scatter(partial_value, 'pcol', scatter_dimension=0, tiled=True)]
    pallas_call x0 -> x1, Pallas kernels: none -> 92.4 us  [shards(): pl.pallas_call(functools.partial(kernel, n_row, n_col, levels, nnz), out_...]
    all_gather x8 -> x0, blocking collectives: 87.2 us -> none  [spread(): return lax.all_gather(solved, 'prow', axis=0, tiled=True)]
    gather x16 -> x0, local copies, waits for them, and re-layouts: 34.3 us -> none  [block_terms(): picked = jnp.take(stored, pointers, axis=0)]
    dot_general x17 -> x0, matrix products: 33.1 us -> none  [the longest x8 23.4 us: block_terms(): jnp.einsum('mkvw,mkwn->mvn', blocks, picked, preferred_element_type=jnp.f...]
    all_gather x7 -> x0, local copies, waits for them, and re-layouts: 7.66 us -> none  [spread(): return lax.all_gather(solved, 'prow', axis=0, tiled=True)]
  transfers between devices with their start and end apart: 8 -> 0, of which waited for: 8 -> 0; matrix products, arithmetic and copies ran while one was open for 0% -> 0% of each run, Pallas kernels for 0% -> 0%
where the time goes in v1:
time: 94.3 us; the launch traced here: 94.2 us
  Pallas kernels  92.4 us (98%)
  local copies, waits for them, and re-layouts  1.72 us (2%)
    pallas_call x1, Pallas kernels, shards(): pl.pallas_call(functools.partial(kernel, n_row, n_col, levels, nnz), out_...  92.4 us

profile of v1, /device:TPU:0, one launch (start us, length us, event | category | flops | bytes accessed | tf_op | source)
XLA Modules:
  0.0 94.2 jit_solution(11609565787884601267)
XLA Ops:
  0.0 92.4 %shard_map.73 = bf16[5,1,128,256]{3,2,1,0:T(8,128)(2,1)} custom-call(bf16[5,1,128,256]{3,2,1,0:T(8,128)(2,1)} %rhs.1, bf16[5,1,128,128]{3,2,1,0:T(8,128)(2,1)} %linv.1, bf16[5,1,128,128]{3,2,1,0:T(8,128)(2,1)} %uinv.1, bf16[4,4,6,128,128]{4,3,2,1,0:T(8,128)(2,1)} %lblk.1, bf16[4,4,6,128,128]{4,3,2,1,0:T(8,128)(2,1)} %ublk.1, s32[4,4,6]{2,1,0:T(4,128)} %lidx.1, ...), custom_call_target="tpu_custom_call" | custom-call | flops 1610612736 | bytes 6291456 | tf_op jit(solution)/shard_map/pallas_call | solution.py:209
  92.4 1.7 %copy.9 = bf16[5,1,128,256]{3,2,1,0:T(8,128)(2,1)} copy(bf16[5,1,128,256]{3,2,1,0:T(8,128)(2,1)} %shard_map.73) | data formatting | bytes 655360

commit v2 on v1

--- a/solution.py
+++ b/solution.py
@@ -22,9 +22,9 @@
 
 def kernel(
     n_row, n_col, levels, nnz,
-    rhs, linv, uinv, lblk, ublk, lidx, uidx, out,
-    blk, land, cache, psend, precv, own, fsol,
-    blk_sem, gather_send, gather_recv, relay_send, part_send, part_recv,
+    rhs_hbm, linv_hbm, uinv_hbm, lblk, ublk, lidx, uidx, out_hbm,
+    rhs, linv, uinv, out, blk, land, cache, psend, precv, own, fsol,
+    small_sem, out_sem, blk_sem, gather_send, gather_recv, relay_send, part_send, part_recv,
 ):
     climbs = levels - 1
     turns = 2 * climbs
@@ -33,21 +33,36 @@
     col = lax.axis_index("pcol")
     core = lax.rem(row, 2)
     sibling = flip(row, 1)
-    planes = [flip(row, 2 * j) for j in range(1, n_row // 2)]
+    strides = range(n_row // 2 - 1, 0, -1)
+    far = [flip(row, 2 * j) for j in strides if j & (j - 1)]
+    near = [flip(row, 2 * j) for j in strides if not j & (j - 1)]
+    cross = [flip(row, 2 * j + 1) for j in strides if not j & (j - 1)]
+    relayed = [flip(peer, 1) for peer in far]
+    friends = far + [sibling] + near + cross
     ends = [flip(col, j) for j in range(n_col - 1, 0, -1)]
 
     def block_copy(turn):
         source = lblk.at[turn] if turn < climbs else ublk.at[turns - 1 - turn]
         return pltpu.make_async_copy(source, blk.at[turn], blk_sem.at[turn])
 
-    for turn in range(turns):
-        block_copy(turn).start()
+    smalls = [
+        pltpu.make_async_copy(source, target, small_sem.at[place])
+        for place, (source, target) in enumerate(((linv_hbm, linv), (rhs_hbm, rhs), (uinv_hbm, uinv)))
+    ]
+
+    def out_copy(height):
+        return pltpu.make_async_copy(out.at[height], out_hbm.at[height], out_sem.at[height])
 
     barrier = pltpu.get_barrier_semaphore()
-    for peer in planes + [sibling]:
+    for peer in friends:
         pl.semaphore_signal(barrier, inc=1, device_id=(peer, col), device_id_type=MESH)
     for peer in ends:
         pl.semaphore_signal(barrier, inc=1, device_id=(row, peer), device_id_type=MESH)
+
+    for copy in smalls:
+        copy.start()
+    for turn in range(turns):
+        block_copy(turn).start()
 
     def gather_copy(turn, half, peer):
         return pltpu.make_async_remote_copy(
@@ -107,24 +122,23 @@
 
     def start_gather(turn, half, level, solved):
         land[turn, half, row] = solved
-        for peer in planes:
+        for peer in friends:
             gather_copy(turn, half, peer).start()
-        gather_copy(turn, half, sibling).start()
         cache[half, level * n_row + row] = solved
 
     def finish_gather(turn, half, level):
-        for peer in planes:
+        for peer in far:
             gather_arrival(turn, half, peer).wait_recv()
             relay_copy(turn, half, peer).start()
             cache[half, level * n_row + peer] = land[turn, half, peer]
-        for slot in [sibling] + [flip(peer, 1) for peer in planes]:
+        for slot in [sibling] + near + cross + relayed:
             gather_arrival(turn, half, slot).wait_recv()
             cache[half, level * n_row + slot] = land[turn, half, slot]
 
     def finish_gather_sends(turn, half):
-        for peer in planes + [sibling]:
+        for peer in friends:
             gather_copy(turn, half, peer).wait_send()
-        for peer in planes:
+        for peer in far:
             relay_copy(turn, half, peer).wait_send()
 
     def row_sum(turn, half, index, level, peer):
@@ -177,13 +191,17 @@
             if forward or not last:
                 start_gather(turn + 1, half, height, solved)
             finish_part_sends(turn, half)
+        if last or not forward:
+            out_copy(height).start()
 
     first = []
+    for copy in smalls:
+        copy.wait()
     for half in range(HALVES):
         solved = apply_inverse(linv[0, 0], rhs[0, 0, :, columns(half)])
         fsol[0, half] = solved
         first.append(solved)
-    pl.semaphore_wait(barrier, len(planes) + 1 + len(ends))
+    pl.semaphore_wait(barrier, len(friends) + len(ends))
     for half in range(HALVES):
         start_gather(0, half, 0, first[half])
 
@@ -191,6 +209,8 @@
     step(climbs - 1, True, True)
     lax.fori_loop(climbs, turns - 1, lambda turn, _: step(turn, False, False), None)
     step(turns - 1, False, True)
+    for height in range(levels):
+        out_copy(height).wait()
 
 
 def shards(
@@ -202,16 +222,19 @@
     turns = 2 * climbs
     width = columns // HALVES
     bf16 = jnp.bfloat16
-    vmem = pl.BlockSpec(memory_space=pltpu.VMEM)
     smem = pl.BlockSpec(memory_space=pltpu.SMEM)
     hbm = pl.BlockSpec(memory_space=pl.ANY)
     dma = pltpu.SemaphoreType.DMA
     return pl.pallas_call(
         functools.partial(kernel, n_row, n_col, levels, nnz),
         out_shape=jax.ShapeDtypeStruct(right_side.shape, bf16),
-        in_specs=[vmem, vmem, vmem, hbm, hbm, smem, smem],
-        out_specs=vmem,
+        in_specs=[hbm, hbm, hbm, hbm, hbm, smem, smem],
+        out_specs=hbm,
         scratch_shapes=[
+            pltpu.VMEM(right_side.shape, bf16),
+            pltpu.VMEM(lower_inverse.shape, bf16),
+            pltpu.VMEM(upper_inverse.shape, bf16),
+            pltpu.VMEM(right_side.shape, bf16),
             pltpu.VMEM((turns, rows, nnz, breadth, breadth), bf16),
             pltpu.VMEM((turns, HALVES, n_row, breadth, width), bf16),
             pltpu.VMEM((HALVES, levels * n_row, breadth, width), bf16),
@@ -219,6 +242,8 @@
             pltpu.VMEM((turns, HALVES, n_col, breadth, width), bf16),
             pltpu.VMEM((HALVES, breadth, width), jnp.float32),
             pltpu.VMEM((levels, HALVES, breadth, width), bf16),
+            dma((3,)),
+            dma((levels,)),
             dma((turns,)),
             dma((turns, HALVES, n_row)),
             dma((turns, HALVES, n_row)),

time: 94.3 us -> 93.9 us (level)
  no operation moved by 1% of the time
where the time goes in v2:
time: 93.9 us; the launch traced here: 93.7 us
  Pallas kernels  91.9 us (98%)
  local copies, waits for them, and re-layouts  1.72 us (2%)
    pallas_call x1, Pallas kernels, shards(): pl.pallas_call(functools.partial(kernel, n_row, n_col, levels, nnz), out_...  91.9 us

profile of v2, /device:TPU:0, one launch (start us, length us, event | category | flops | bytes accessed | tf_op | source)
XLA Modules:
  0.0 93.7 jit_solution(13322670789706800521)
XLA Ops:
  0.0 91.9 %shard_map.73 = bf16[5,1,128,256]{3,2,1,0:T(8,128)(2,1)} custom-call(bf16[5,1,128,256]{3,2,1,0:T(8,128)(2,1)} %rhs_hbm.1, bf16[5,1,128,128]{3,2,1,0:T(8,128)(2,1)} %linv_hbm.1, bf16[5,1,128,128]{3,2,1,0:T(8,128)(2,1)} %uinv_hbm.1, bf16[4,4,6,128,128]{4,3,2,1,0:T(8,128)(2,1)} %lblk.1, bf16[4,4,6,128,128]{4,3,2,1,0:T(8,128)(2,1)} %ublk.1, s32[4,4,6]{2,1,0:T(4,128)} %lidx.1, ...), custom_call_target="tpu_custom_call" | custom-call | flops 1610612736 | bytes 6291456 | tf_op jit(solution)/shard_map/pallas_call | solution.py:228
  92.0 1.7 %copy.9 = bf16[5,1,128,256]{3,2,1,0:T(8,128)(2,1)} copy(bf16[5,1,128,256]{3,2,1,0:T(8,128)(2,1)} %shard_map.73) | data formatting | bytes 655360

commit v3 on v2

--- a/solution.py
+++ b/solution.py
@@ -23,7 +23,7 @@
 def kernel(
     n_row, n_col, levels, nnz,
     rhs_hbm, linv_hbm, uinv_hbm, lblk, ublk, lidx, uidx, out_hbm,
-    rhs, linv, uinv, out, blk, land, cache, psend, precv, own, fsol,
+    rhs, linv, uinv, out, blk, land, cache, psend, precv, own, held, fsol,
     small_sem, out_sem, blk_sem, gather_send, gather_recv, relay_send, part_send, part_recv,
 ):
     climbs = levels - 1
@@ -34,12 +34,14 @@
     core = lax.rem(row, 2)
     sibling = flip(row, 1)
     strides = range(n_row // 2 - 1, 0, -1)
-    far = [flip(row, 2 * j) for j in strides if j & (j - 1)]
-    near = [flip(row, 2 * j) for j in strides if not j & (j - 1)]
-    cross = [flip(row, 2 * j + 1) for j in strides if not j & (j - 1)]
-    relayed = [flip(peer, 1) for peer in far]
-    friends = far + [sibling] + near + cross
-    ends = [flip(col, j) for j in range(n_col - 1, 0, -1)]
+    planes = [flip(row, 2 * j) for j in strides]
+    relayed = [flip(peer, 1) for peer in planes]
+    friends = planes + [sibling]
+    folded = n_col == 4
+    ends = [flip(col, j) for j in range(n_col)]
+    outer = (col == 0) | (col == n_col - 1)
+    inner = jnp.logical_not(outer)
+    order = (2, 3, 1) if folded else range(n_col - 1, 0, -1)
 
     def block_copy(turn):
         source = lblk.at[turn] if turn < climbs else ublk.at[turns - 1 - turn]
@@ -56,7 +58,7 @@
     barrier = pltpu.get_barrier_semaphore()
     for peer in friends:
         pl.semaphore_signal(barrier, inc=1, device_id=(peer, col), device_id_type=MESH)
-    for peer in ends:
+    for peer in ends[1:]:
         pl.semaphore_signal(barrier, inc=1, device_id=(row, peer), device_id_type=MESH)
 
     for copy in smalls:
@@ -94,22 +96,13 @@
             device_id_type=MESH,
         )
 
-    def part_copy(turn, half, peer):
+    def part_copy(turn, half, j):
+        peer = jnp.where(outer, ends[1], ends[2]) if folded and j == 2 else ends[j]
         return pltpu.make_async_remote_copy(
-            src_ref=psend.at[turn, half, peer],
-            dst_ref=precv.at[turn, half, col],
-            send_sem=part_send.at[turn, half, peer],
-            recv_sem=part_recv.at[turn, half, col],
-            device_id=(row, peer),
-            device_id_type=MESH,
-        )
-
-    def part_arrival(turn, half, peer):
-        return pltpu.make_async_remote_copy(
-            src_ref=psend.at[turn, half, peer],
-            dst_ref=precv.at[turn, half, peer],
-            send_sem=part_send.at[turn, half, peer],
-            recv_sem=part_recv.at[turn, half, peer],
+            src_ref=psend.at[turn, half, j],
+            dst_ref=precv.at[turn, half, j],
+            send_sem=part_send.at[turn, half, j],
+            recv_sem=part_recv.at[turn, half, j],
             device_id=(row, peer),
             device_id_type=MESH,
         )
@@ -127,18 +120,18 @@
         cache[half, level * n_row + row] = solved
 
     def finish_gather(turn, half, level):
-        for peer in far:
+        for peer in planes:
             gather_arrival(turn, half, peer).wait_recv()
             relay_copy(turn, half, peer).start()
             cache[half, level * n_row + peer] = land[turn, half, peer]
-        for slot in [sibling] + near + cross + relayed:
+        for slot in [sibling] + relayed:
             gather_arrival(turn, half, slot).wait_recv()
             cache[half, level * n_row + slot] = land[turn, half, slot]
 
     def finish_gather_sends(turn, half):
         for peer in friends:
             gather_copy(turn, half, peer).wait_send()
-        for peer in far:
+        for peer in planes:
             relay_copy(turn, half, peer).wait_send()
 
     def row_sum(turn, half, index, level, peer):
@@ -149,21 +142,43 @@
         return jnp.dot(left, right, preferred_element_type=jnp.float32)
 
     def send_parts(turn, half, index, level):
-        for peer in ends:
-            psend[turn, half, peer] = row_sum(turn, half, index, level, peer).astype(jnp.bfloat16)
-            part_copy(turn, half, peer).start()
+        for j in order:
+            value = row_sum(turn, half, index, level, ends[j])
+            if folded and j == 3:
+                held[half] = value
+
+                @pl.when(outer)
+                def _():
+                    psend[turn, half, j] = held[half].astype(jnp.bfloat16)
+                    part_copy(turn, half, j).start()
+            else:
+                psend[turn, half, j] = value.astype(jnp.bfloat16)
+                part_copy(turn, half, j).start()
         own[half] = row_sum(turn, half, index, level, col)
 
+    def fold_parts(turn, half):
+        @pl.when(inner)
+        def _():
+            part_copy(turn, half, 2).wait_recv()
+            value = held[half] + precv[turn, half, 2].astype(jnp.float32)
+            psend[turn, half, 3] = value.astype(jnp.bfloat16)
+            part_copy(turn, half, 3).start()
+
     def take_parts(turn, half):
-        total = own[half]
-        for peer in ends[::-1]:
-            part_arrival(turn, half, peer).wait_recv()
-            total = total + precv[turn, half, peer].astype(jnp.float32)
-        return total
+        for j in order[::-1]:
+            if folded and j == 2:
+                @pl.when(outer)
+                def _():
+                    part_copy(turn, half, j).wait_recv()
+                    own[half] += precv[turn, half, j].astype(jnp.float32)
+            else:
+                part_copy(turn, half, j).wait_recv()
+                own[half] += precv[turn, half, j].astype(jnp.float32)
+        return own[half]
 
     def finish_part_sends(turn, half):
-        for peer in ends:
-            part_copy(turn, half, peer).wait_send()
+        for j in order:
+            part_copy(turn, half, j).wait_send()
 
     def step(turn, forward, last):
         before = turn if forward else turns - turn
@@ -173,6 +188,8 @@
         for half in range(HALVES):
             finish_gather(turn, half, before)
             send_parts(turn, half, index, level)
+            if folded:
+                fold_parts(turn, half)
         for half in range(HALVES):
             finish_gather_sends(turn, half)
             total = take_parts(turn, half)
@@ -201,7 +218,7 @@
         solved = apply_inverse(linv[0, 0], rhs[0, 0, :, columns(half)])
         fsol[0, half] = solved
         first.append(solved)
-    pl.semaphore_wait(barrier, len(friends) + len(ends))
+    pl.semaphore_wait(barrier, len(friends) + n_col - 1)
     for half in range(HALVES):
         start_gather(0, half, 0, first[half])
 
@@ -241,6 +258,7 @@
             pltpu.VMEM((turns, HALVES, n_col, breadth, width), bf16),
             pltpu.VMEM((turns, HALVES, n_col, breadth, width), bf16),
             pltpu.VMEM((HALVES, breadth, width), jnp.float32),
+            pltpu.VMEM((HALVES, breadth, width), jnp.float32),
             pltpu.VMEM((levels, HALVES, breadth, width), bf16),
             dma((3,)),
             dma((levels,)),

time: 93.9 us -> 96.8 us (1.031)
  Pallas kernels: 91.9 us -> 94.9 us
    pallas_call x1, Pallas kernels: 91.9 us -> 94.9 us  [shards(): pl.pallas_call(functools.partial(kernel, n_row, n_col, levels, nnz), out_...]
where the time goes in v3:
time: 96.8 us; the launch traced here: 96.6 us
  Pallas kernels  94.9 us (98%)
  local copies, waits for them, and re-layouts  1.72 us (2%)
    pallas_call x1, Pallas kernels, shards(): pl.pallas_call(functools.partial(kernel, n_row, n_col, levels, nnz), out_...  94.9 us

profile of v3, /device:TPU:0, one launch (start us, length us, event | category | flops | bytes accessed | tf_op | source)
XLA Modules:
  0.0 96.6 jit_solution(13264132774566311078)
XLA Ops:
  0.0 94.9 %shard_map.73 = bf16[5,1,128,256]{3,2,1,0:T(8,128)(2,1)} custom-call(bf16[5,1,128,256]{3,2,1,0:T(8,128)(2,1)} %rhs_hbm.1, bf16[5,1,128,128]{3,2,1,0:T(8,128)(2,1)} %linv_hbm.1, bf16[5,1,128,128]{3,2,1,0:T(8,128)(2,1)} %uinv_hbm.1, bf16[4,4,6,128,128]{4,3,2,1,0:T(8,128)(2,1)} %lblk.1, bf16[4,4,6,128,128]{4,3,2,1,0:T(8,128)(2,1)} %ublk.1, s32[4,4,6]{2,1,0:T(4,128)} %lidx.1, ...), custom_call_target="tpu_custom_call" | custom-call | flops 1610612736 | bytes 6291456 | tf_op jit(solution)/shard_map/pallas_call | solution.py:245
  94.9 1.7 %copy.9 = bf16[5,1,128,256]{3,2,1,0:T(8,128)(2,1)} copy(bf16[5,1,128,256]{3,2,1,0:T(8,128)(2,1)} %shard_map.73) | data formatting | bytes 655360

commit v4 on v3

--- a/solution.py
+++ b/solution.py
@@ -8,7 +8,7 @@
 from jax.sharding import PartitionSpec as P
 
 MESH = pl.DeviceIdType.MESH
-HALVES = 2
+HALVES = 1
 
 
 def flip(index, bits):
@@ -37,7 +37,7 @@
     planes = [flip(row, 2 * j) for j in strides]
     relayed = [flip(peer, 1) for peer in planes]
     friends = planes + [sibling]
-    folded = n_col == 4
+    folded = False
     ends = [flip(col, j) for j in range(n_col)]
     outer = (col == 0) | (col == n_col - 1)
     inner = jnp.logical_not(outer)

time: 96.8 us -> 118 us (1.22)
  Pallas kernels: 94.9 us -> 116 us
    pallas_call x1, Pallas kernels: 94.9 us -> 116 us  [shards(): pl.pallas_call(functools.partial(kernel, n_row, n_col, levels, nnz), out_...]
where the time goes in v4:
time: 118 us
  Pallas kernels  116 us (98%)
  local copies, waits for them, and re-layouts  1.72 us (1%)
    pallas_call x1, Pallas kernels, shards(): pl.pallas_call(functools.partial(kernel, n_row, n_col, levels, nnz), out_...  116 us

profile of v4, /device:TPU:0, one launch (start us, length us, event | category | flops | bytes accessed | tf_op | source)
XLA Modules:
  0.0 117.9 jit_solution(10654854204457262391)
XLA Ops:
  0.0 116.1 %shard_map.73 = bf16[5,1,128,256]{3,2,1,0:T(8,128)(2,1)} custom-call(bf16[5,1,128,256]{3,2,1,0:T(8,128)(2,1)} %rhs_hbm.1, bf16[5,1,128,128]{3,2,1,0:T(8,128)(2,1)} %linv_hbm.1, bf16[5,1,128,128]{3,2,1,0:T(8,128)(2,1)} %uinv_hbm.1, bf16[4,4,6,128,128]{4,3,2,1,0:T(8,128)(2,1)} %lblk.1, bf16[4,4,6,128,128]{4,3,2,1,0:T(8,128)(2,1)} %ublk.1, s32[4,4,6]{2,1,0:T(4,128)} %lidx.1, ...), custom_call_target="tpu_custom_call" | custom-call | flops 1610612736 | bytes 6291456 | tf_op jit(solution)/shard_map/pallas_call | solution.py:245
  116.1 1.7 %copy.9 = bf16[5,1,128,256]{3,2,1,0:T(8,128)(2,1)} copy(bf16[5,1,128,256]{3,2,1,0:T(8,128)(2,1)} %shard_map.73) | data formatting | bytes 655360

commit v5 on v2

v5 whole, which is shorter than its diff:
```python
import functools

import jax
import jax.numpy as jnp
from jax import lax
from jax.experimental import pallas as pl
from jax.experimental.pallas import tpu as pltpu
from jax.sharding import PartitionSpec as P

MESH = pl.DeviceIdType.MESH
PIECES = 4


def flip(index, bits):
    bit = 1
    while bit <= bits:
        if bits & bit:
            index = index + bit - 2 * bit * lax.rem(lax.div(index, bit), 2)
        bit *= 2
    return index


def pack(piece):
    count = max(1, 128 // piece.shape[1])
    rows = piece.shape[0] // count
    return jnp.concatenate([piece[i * rows:(i + 1) * rows] for i in range(count)], axis=1)


def unpack(packed, width):
    return jnp.concatenate(
        [packed[:, i:i + width] for i in range(0, packed.shape[1], width)], axis=0
    )


def kernel(
    n_row, n_col, levels, nnz,
    rhs_hbm, linv_hbm, uinv_hbm, lblk, ublk, lidx, uidx, out_hbm,
    rhs, linv, uinv, out, blk, land, cache, psend, precv, own, fsol,
    small_sem, out_sem, blk_sem, gather_send, gather_recv, relay_send, part_send, part_recv,
):
    climbs = levels - 1
    turns = 2 * climbs
    width = cache.shape[-1]
    row = lax.axis_index("prow")
    col = lax.axis_index("pcol")
    core = lax.rem(row, 2)
    sibling = flip(row, 1)
    strides = range(n_row // 2 - 1, 0, -1)
    far = [flip(row, 2 * j) for j in strides if j & (j - 1)]
    near = [flip(row, 2 * j) for j in strides if not j & (j - 1)]
    cross = [flip(row, 2 * j + 1) for j in strides if not j & (j - 1)]
    relayed = [flip(peer, 1) for peer in far]
    friends = far + [sibling] + near + cross
    ends = [flip(col, j) for j in range(n_col - 1, 0, -1)]

    def block_copy(turn):
        source = lblk.at[turn] if turn < climbs else ublk.at[turns - 1 - turn]
        return pltpu.make_async_copy(source, blk.at[turn], blk_sem.at[turn])

    smalls = [
        pltpu.make_async_copy(source, target, small_sem.at[place])
        for place, (source, target) in enumerate(((linv_hbm, linv), (rhs_hbm, rhs), (uinv_hbm, uinv)))
    ]

    def out_copy(height):
        return pltpu.make_async_copy(out.at[height], out_hbm.at[height], out_sem.at[height])

    barrier = pltpu.get_barrier_semaphore()
    for peer in friends:
        pl.semaphore_signal(barrier, inc=1, device_id=(peer, col), device_id_type=MESH)
    for peer in ends:
        pl.semaphore_signal(barrier, inc=1, device_id=(row, peer), device_id_type=MESH)

    for copy in smalls:
        copy.start()
    for turn in range(turns):
        block_copy(turn).start()

    def gather_copy(turn, piece, peer):
        return pltpu.make_async_remote_copy(
            src_ref=land.at[turn, piece, row],
            dst_ref=land.at[turn, piece, row],
            send_sem=gather_send.at[turn, piece, peer],
            recv_sem=gather_recv.at[turn, piece, row],
            device_id=(peer, col),
            device_id_type=MESH,
        )

    def gather_arrival(turn, piece, slot):
        return pltpu.make_async_remote_copy(
            src_ref=land.at[turn, piece, slot],
            dst_ref=land.at[turn, piece, slot],
            send_sem=gather_send.at[turn, piece, slot],
            recv_sem=gather_recv.at[turn, piece, slot],
            device_id=(sibling, col),
            device_id_type=MESH,
        )

    def relay_copy(turn, piece, slot):
        return pltpu.make_async_remote_copy(
            src_ref=land.at[turn, piece, slot],
            dst_ref=land.at[turn, piece, slot],
            send_sem=relay_send.at[turn, piece, lax.div(slot, 2)],
            recv_sem=gather_recv.at[turn, piece, slot],
            device_id=(sibling, col),
            device_id_type=MESH,
        )

    def part_copy(turn, piece, peer):
        return pltpu.make_async_remote_copy(
            src_ref=psend.at[turn, piece, peer],
            dst_ref=precv.at[turn, piece, col],
            send_sem=part_send.at[turn, piece, peer],
            recv_sem=part_recv.at[turn, piece, col],
            device_id=(row, peer),
            device_id_type=MESH,
        )

    def part_arrival(turn, piece, peer):
        return pltpu.make_async_remote_copy(
            src_ref=psend.at[turn, piece, peer],
            dst_ref=precv.at[turn, piece, peer],
            send_sem=part_send.at[turn, piece, peer],
            recv_sem=part_recv.at[turn, piece, peer],
            device_id=(row, peer),
            device_id_type=MESH,
        )

    def columns(piece):
        return slice(piece * width, (piece + 1) * width)

    def apply_inverse(inverse, remain):
        return jnp.dot(inverse, remain, preferred_element_type=jnp.float32)

    def start_gather(turn, piece, level, solved):
        land[turn, piece, row] = pack(solved).astype(jnp.bfloat16)
        for peer in friends:
            gather_copy(turn, piece, peer).start()
        cache[piece, level * n_row + row] = solved.astype(jnp.bfloat16)

    def finish_gather(turn, piece, level):
        for peer in far:
            gather_arrival(turn, piece, peer).wait_recv()
            relay_copy(turn, piece, peer).start()
            cache[piece, level * n_row + peer] = unpack(land[turn, piece, peer], width)
        for slot in [sibling] + near + cross + relayed:
            gather_arrival(turn, piece, slot).wait_recv()
            cache[piece, level * n_row + slot] = unpack(land[turn, piece, slot], width)

    def finish_gather_sends(turn, piece):
        for peer in friends:
            gather_copy(turn, piece, peer).wait_send()
        for peer in far:
            relay_copy(turn, piece, peer).wait_send()

    def row_sum(turn, piece, index, level, peer):
        left = jnp.concatenate([blk[turn, peer, k] for k in range(nnz)], axis=1)
        right = jnp.concatenate(
            [cache[piece, index[level, peer, k]] for k in range(nnz)], axis=0
        )
        return jnp.dot(left, right, preferred_element_type=jnp.float32)

    def send_parts(turn, piece, index, level):
        for peer in ends:
            psend[turn, piece, peer] = pack(row_sum(turn, piece, index, level, peer)).astype(jnp.bfloat16)
            part_copy(turn, piece, peer).start()
        own[piece] = pack(row_sum(turn, piece, index, level, col))

    def take_parts(turn, piece):
        total = own[piece]
        for peer in ends[::-1]:
            part_arrival(turn, piece, peer).wait_recv()
            total = total + precv[turn, piece, peer].astype(jnp.float32)
        return unpack(total, width)

    def finish_part_sends(turn, piece):
        for peer in ends:
            part_copy(turn, piece, peer).wait_send()

    def step(turn, forward, last):
        before = turn if forward else turns - turn
        height = turn + 1 if forward else turns - 1 - turn
        index, level = (lidx, turn) if forward else (uidx, height)
        pltpu.make_async_copy(lblk.at[0], blk.at[turn], blk_sem.at[turn]).wait()
        for piece in range(PIECES):
            finish_gather(turn, piece, before)
            send_parts(turn, piece, index, level)
        for piece in range(PIECES):
            finish_gather_sends(turn, piece)
            source = rhs[height, 0, :, columns(piece)] if forward else fsol[height, piece]
            source = source.astype(jnp.float32)
            remain = (source - take_parts(turn, piece)).astype(jnp.bfloat16)
            solved = apply_inverse(linv[height, 0] if forward else uinv[height, 0], remain)
            if forward and last:
                solved = apply_inverse(uinv[height, 0], solved.astype(jnp.bfloat16))
            if forward or not last:
                start_gather(turn + 1, piece, height, solved)
            if last or not forward:
                out[height, 0, :, columns(piece)] = solved.astype(jnp.bfloat16)
            else:
                fsol[height, piece] = solved.astype(jnp.bfloat16)
            finish_part_sends(turn, piece)
        if last or not forward:
            out_copy(height).start()

    first = []
    for copy in smalls:
        copy.wait()
    for piece in range(PIECES):
        solved = apply_inverse(linv[0, 0], rhs[0, 0, :, columns(piece)])
        fsol[0, piece] = solved.astype(jnp.bfloat16)
        first.append(solved)
    pl.semaphore_wait(barrier, len(friends) + len(ends))
    for piece in range(PIECES):
        start_gather(0, piece, 0, first[piece])

    lax.fori_loop(0, climbs - 1, lambda turn, _: step(turn, True, False), None)
    step(climbs - 1, True, True)
    lax.fori_loop(climbs, turns - 1, lambda turn, _: step(turn, False, False), None)
    step(turns - 1, False, True)
    for height in range(levels):
        out_copy(height).wait()


def shards(
    right_side, lower_inverse, upper_inverse, lower_blocks, lower_index, upper_blocks, upper_index
):
    n_row, n_col = lax.axis_size("prow"), lax.axis_size("pcol")
    levels, _, breadth, columns = right_side.shape
    climbs, rows, nnz = lower_index.shape
    turns = 2 * climbs
    width = columns // PIECES
    packed = (breadth * width // 128, 128)
    bf16 = jnp.bfloat16
    smem = pl.BlockSpec(memory_space=pltpu.SMEM)
    hbm = pl.BlockSpec(memory_space=pl.ANY)
    dma = pltpu.SemaphoreType.DMA
    return pl.pallas_call(
        functools.partial(kernel, n_row, n_col, levels, nnz),
        out_shape=jax.ShapeDtypeStruct(right_side.shape, bf16),
        in_specs=[hbm, hbm, hbm, hbm, hbm, smem, smem],
        out_specs=hbm,
        scratch_shapes=[
            pltpu.VMEM(right_side.shape, bf16),
            pltpu.VMEM(lower_inverse.shape, bf16),
            pltpu.VMEM(upper_inverse.shape, bf16),
            pltpu.VMEM(right_side.shape, bf16),
            pltpu.VMEM((turns, rows, nnz, breadth, breadth), bf16),
            pltpu.VMEM((turns, PIECES, n_row) + packed, bf16),
            pltpu.VMEM((PIECES, levels * n_row, breadth, width), bf16),
            pltpu.VMEM((turns, PIECES, n_col) + packed, bf16),
            pltpu.VMEM((turns, PIECES, n_col) + packed, bf16),
            pltpu.VMEM((PIECES,) + packed, jnp.float32),
            pltpu.VMEM((levels, PIECES, breadth, width), bf16),
            dma((3,)),
            dma((levels,)),
            dma((turns,)),
            dma((turns, PIECES, n_row)),
            dma((turns, PIECES, n_row)),
            dma((turns, PIECES, n_row // 2)),
            dma((turns, PIECES, n_col)),
            dma((turns, PIECES, n_col)),
        ],
        compiler_params=pltpu.CompilerParams(
            collective_id=0, has_side_effects=True, vmem_limit_bytes=62 * 1024 * 1024
        ),
        cost_estimate=pl.CostEstimate(
            flops=2 * turns * rows * nnz * breadth * breadth * columns,
            bytes_accessed=2 * turns * rows * nnz * breadth * breadth,
            transcendentals=0,
        ),
    )(
        right_side, lower_inverse, upper_inverse,
        lower_blocks, upper_blocks, lower_index, upper_index,
    )


def solution(mesh):
    placed = (
        P(None, ("prow", "pcol"), None, None),
        P(None, ("prow", "pcol"), None, None),
        P(None, ("prow", "pcol"), None, None),
        P(None, "prow", "pcol", None, None),
        P(None, "prow", "pcol"),
        P(None, "prow", "pcol", None, None),
        P(None, "prow", "pcol"),
    )
    return jax.shard_map(
        shards,
        mesh=mesh,
        in_specs=placed,
        out_specs=P(None, ("prow", "pcol"), None, None),
        check_vma=False,
    )
```

time: 93.9 us -> 120 us (1.28)
  Pallas kernels: 91.9 us -> 118 us
    pallas_call x1, Pallas kernels: 91.9 us -> 118 us  [shards(): pl.pallas_call(functools.partial(kernel, n_row, n_col, levels, nnz), out_...]
where the time goes in v5:
time: 120 us; the launch traced here: 119 us
  Pallas kernels  118 us (98%)
  local copies, waits for them, and re-layouts  1.72 us (1%)
    pallas_call x1, Pallas kernels, shards(): pl.pallas_call(functools.partial(kernel, n_row, n_col, levels, nnz), out_...  118 us

profile of v5, /device:TPU:0, one launch (start us, length us, event | category | flops | bytes accessed | tf_op | source)
XLA Modules:
  0.0 119.3 jit_solution(8815684944438761865)
XLA Ops:
  0.0 117.6 %shard_map.73 = bf16[5,1,128,256]{3,2,1,0:T(8,128)(2,1)} custom-call(bf16[5,1,128,256]{3,2,1,0:T(8,128)(2,1)} %rhs_hbm.1, bf16[5,1,128,128]{3,2,1,0:T(8,128)(2,1)} %linv_hbm.1, bf16[5,1,128,128]{3,2,1,0:T(8,128)(2,1)} %uinv_hbm.1, bf16[4,4,6,128,128]{4,3,2,1,0:T(8,128)(2,1)} %lblk.1, bf16[4,4,6,128,128]{4,3,2,1,0:T(8,128)(2,1)} %ublk.1, s32[4,4,6]{2,1,0:T(4,128)} %lidx.1, ...), custom_call_target="tpu_custom_call" | custom-call | flops 1610612736 | bytes 6291456 | tf_op jit(solution)/shard_map/pallas_call | solution.py:238
  117.6 1.7 %copy.9 = bf16[5,1,128,256]{3,2,1,0:T(8,128)(2,1)} copy(bf16[5,1,128,256]{3,2,1,0:T(8,128)(2,1)} %shard_map.73) | data formatting | bytes 655360

commit v6 on v5

v6 whole, which is shorter than its diff:
```python
import functools

import jax
import jax.numpy as jnp
from jax import lax
from jax.experimental import pallas as pl
from jax.experimental.pallas import tpu as pltpu
from jax.sharding import PartitionSpec as P

MESH = pl.DeviceIdType.MESH
PIECES = 2


def flip(index, bits):
    bit = 1
    while bit <= bits:
        if bits & bit:
            index = index + bit - 2 * bit * lax.rem(lax.div(index, bit), 2)
        bit *= 2
    return index


def kernel(
    n_row, n_col, levels, nnz,
    rhs_hbm, linv_hbm, uinv_hbm, lblk, ublk, lidx, uidx, out_hbm,
    rhs, linv, uinv, out, blk, land, cache, psend, precv, own, fsol,
    small_sem, out_sem, blk_sem, gather_send, gather_recv, far_recv, relay_send, part_send, part_recv,
):
    climbs = levels - 1
    turns = 2 * climbs
    width = land.shape[-1]
    row = lax.axis_index("prow")
    col = lax.axis_index("pcol")
    core = lax.rem(row, 2)
    sibling = flip(row, 1)
    strides = range(n_row // 2 - 1, 0, -1)
    far = [flip(row, 2 * j) for j in strides if j & (j - 1)]
    near = [flip(row, 2 * j) for j in strides if not j & (j - 1)]
    cross = [flip(row, 2 * j + 1) for j in strides if not j & (j - 1)]
    relayed = [flip(peer, 1) for peer in far]
    friends = far + [sibling] + near + cross
    ends = [flip(col, j) for j in range(1, n_col)]

    def block_copy(turn):
        source = lblk.at[turn] if turn < climbs else ublk.at[turns - 1 - turn]
        return pltpu.make_async_copy(source, blk.at[turn], blk_sem.at[turn])

    smalls = [
        pltpu.make_async_copy(source, target, small_sem.at[place])
        for place, (source, target) in enumerate(((linv_hbm, linv), (rhs_hbm, rhs), (uinv_hbm, uinv)))
    ]

    def out_copy(height):
        return pltpu.make_async_copy(out.at[height], out_hbm.at[height], out_sem.at[height])

    barrier = pltpu.get_barrier_semaphore()
    for peer in friends:
        pl.semaphore_signal(barrier, inc=1, device_id=(peer, col), device_id_type=MESH)
    for peer in ends:
        pl.semaphore_signal(barrier, inc=1, device_id=(row, peer), device_id_type=MESH)

    for copy in smalls:
        copy.start()
    for turn in range(turns):
        block_copy(turn).start()

    def remote(source, target, send_sem, recv_sem, device):
        return pltpu.make_async_remote_copy(
            src_ref=source, dst_ref=target, send_sem=send_sem, recv_sem=recv_sem,
            device_id=device, device_id_type=MESH,
        )

    def arrival(target, sem):
        return remote(target, target, sem, sem, (sibling, col))

    def relay_copy(turn, piece, peer):
        slot = land.at[turn, piece, peer]
        return remote(
            slot, slot, relay_send.at[turn, piece], gather_recv.at[turn, piece], (sibling, col)
        )

    def part_copy(turn, piece, j):
        return remote(
            psend.at[turn, piece, j], precv.at[turn, piece, j],
            part_send.at[turn, piece], part_recv.at[turn, piece], (row, ends[j]),
        )

    def columns(piece):
        return pl.ds(pl.multiple_of(piece * width, width), width)

    def apply_inverse(inverse, remain):
        return jnp.dot(inverse, remain, preferred_element_type=jnp.float32).astype(jnp.bfloat16)

    def start_gather(turn, piece):
        slot = land.at[turn, piece, row]
        for i, peer in enumerate(far):
            remote(
                slot, slot, gather_send.at[turn, piece], far_recv.at[turn, piece, i], (peer, col)
            ).start()
        for peer in friends[len(far):]:
            remote(
                slot, slot, gather_send.at[turn, piece], gather_recv.at[turn, piece], (peer, col)
            ).start()

    def finish_gather(turn, piece, level):
        for i, peer in enumerate(far):
            arrival(land.at[turn, piece, peer], far_recv.at[turn, piece, i]).wait_recv()
            relay_copy(turn, piece, peer).start()
        rest = n_row - 1 - len(far)
        arrival(land.at[turn, piece, pl.ds(0, rest)], gather_recv.at[turn, piece]).wait_recv()
        cache[piece, pl.ds(level * n_row, n_row)] = land[turn, piece]

    def finish_gather_sends(turn, piece):
        sent = land.at[turn, piece, pl.ds(0, len(friends))]
        arrival(sent, gather_send.at[turn, piece]).wait_send()
        if far:
            sent = land.at[turn, piece, pl.ds(0, len(far))]
            arrival(sent, relay_send.at[turn, piece]).wait_send()

    def row_sum(turn, piece, index, level, peer):
        left = jnp.concatenate([blk[turn, peer, k] for k in range(nnz)], axis=1)
        right = jnp.concatenate(
            [cache[piece, index[level, peer, k]] for k in range(nnz)], axis=0
        )
        return jnp.dot(left, right, preferred_element_type=jnp.float32)

    def send_parts(turn, piece, index, level):
        for j in range(len(ends) - 1, -1, -1):
            value = row_sum(turn, piece, index, level, ends[j])
            psend[turn, piece, j] = value.astype(jnp.bfloat16)
            part_copy(turn, piece, j).start()
        own[piece] = row_sum(turn, piece, index, level, col)

    def take_parts(turn, piece):
        arrival(precv.at[turn, piece], part_recv.at[turn, piece]).wait_recv()
        total = own[piece]
        for j in range(len(ends)):
            total = total + precv[turn, piece, j].astype(jnp.float32)
        return total

    def step(turn, forward):
        before = turn if forward else turns - turn
        height = turn + 1 if forward else turns - 1 - turn
        index, level = (lidx, turn) if forward else (uidx, height)
        pltpu.make_async_copy(lblk.at[0], blk.at[turn], blk_sem.at[turn]).wait()

        def spread(piece, _):
            finish_gather(turn, piece, before)
            send_parts(turn, piece, index, level)

        def settle(piece, _):
            finish_gather_sends(turn, piece)
            source = rhs[height, 0, :, columns(piece)] if forward else fsol[height, piece]
            total = take_parts(turn, piece)
            remain = (source.astype(jnp.float32) - total).astype(jnp.bfloat16)
            if forward:
                solved = apply_inverse(linv[height, 0], remain)

                @pl.when(turn < climbs - 1)
                def _():
                    land[turn + 1, piece, row] = solved
                    fsol[height, piece] = solved

                @pl.when(turn == climbs - 1)
                def _():
                    top = apply_inverse(uinv[height, 0], solved)
                    land[turn + 1, piece, row] = top
                    out[height, 0, :, columns(piece)] = top

                start_gather(turn + 1, piece)
            else:
                solved = apply_inverse(uinv[height, 0], remain)

                @pl.when(turn < turns - 1)
                def _():
                    land[turn + 1, piece, row] = solved
                    start_gather(turn + 1, piece)

                out[height, 0, :, columns(piece)] = solved
            arrival(psend.at[turn, piece], part_send.at[turn, piece]).wait_send()

        lax.fori_loop(0, PIECES, spread, None)
        lax.fori_loop(0, PIECES, settle, None)
        if forward:
            @pl.when(turn == climbs - 1)
            def _():
                out_copy(height).start()
        else:
            out_copy(height).start()

    for copy in smalls:
        copy.wait()

    def begin(piece, _):
        solved = apply_inverse(linv[0, 0], rhs[0, 0, :, columns(piece)])
        land[0, piece, row] = solved
        fsol[0, piece] = solved

    lax.fori_loop(0, PIECES, begin, None)
    pl.semaphore_wait(barrier, len(friends) + len(ends))
    for piece in range(PIECES):
        start_gather(0, piece)

    lax.fori_loop(0, climbs, lambda turn, _: step(turn, True), None)
    lax.fori_loop(climbs, turns, lambda turn, _: step(turn, False), None)
    for height in range(levels):
        out_copy(height).wait()


def shards(
    right_side, lower_inverse, upper_inverse, lower_blocks, lower_index, upper_blocks, upper_index
):
    n_row, n_col = lax.axis_size("prow"), lax.axis_size("pcol")
    levels, _, breadth, columns = right_side.shape
    climbs, rows, nnz = lower_index.shape
    turns = 2 * climbs
    width = columns // PIECES
    bf16 = jnp.bfloat16
    smem = pl.BlockSpec(memory_space=pltpu.SMEM)
    hbm = pl.BlockSpec(memory_space=pl.ANY)
    dma = pltpu.SemaphoreType.DMA
    return pl.pallas_call(
        functools.partial(kernel, n_row, n_col, levels, nnz),
        out_shape=jax.ShapeDtypeStruct(right_side.shape, bf16),
        in_specs=[hbm, hbm, hbm, hbm, hbm, smem, smem],
        out_specs=hbm,
        scratch_shapes=[
            pltpu.VMEM(right_side.shape, bf16),
            pltpu.VMEM(lower_inverse.shape, bf16),
            pltpu.VMEM(upper_inverse.shape, bf16),
            pltpu.VMEM(right_side.shape, bf16),
            pltpu.VMEM((turns, rows, nnz, breadth, breadth), bf16),
            pltpu.VMEM((turns, PIECES, n_row, breadth, width), bf16),
            pltpu.VMEM((PIECES, levels * n_row, breadth, width), bf16),
            pltpu.VMEM((turns, PIECES, n_col - 1, breadth, width), bf16),
            pltpu.VMEM((turns, PIECES, n_col - 1, breadth, width), bf16),
            pltpu.VMEM((PIECES, breadth, width), jnp.float32),
            pltpu.VMEM((levels, PIECES, breadth, width), bf16),
            dma((3,)),
            dma((levels,)),
            dma((turns,)),
            dma((turns, PIECES)),
            dma((turns, PIECES)),
            dma((turns, PIECES, max(1, n_row // 2))),
            dma((turns, PIECES)),
            dma((turns, PIECES)),
            dma((turns, PIECES)),
        ],
        compiler_params=pltpu.CompilerParams(
            collective_id=0, has_side_effects=True, vmem_limit_bytes=58 * 1024 * 1024
        ),
        cost_estimate=pl.CostEstimate(
            flops=2 * turns * rows * nnz * breadth * breadth * columns,
            bytes_accessed=2 * turns * rows * nnz * breadth * breadth,
            transcendentals=0,
        ),
    )(
        right_side, lower_inverse, upper_inverse,
        lower_blocks, upper_blocks, lower_index, upper_index,
    )


def solution(mesh):
    placed = (
        P(None, ("prow", "pcol"), None, None),
        P(None, ("prow", "pcol"), None, None),
        P(None, ("prow", "pcol"), None, None),
        P(None, "prow", "pcol", None, None),
        P(None, "prow", "pcol"),
        P(None, "prow", "pcol", None, None),
        P(None, "prow", "pcol"),
    )
    return jax.shard_map(
        shards,
        mesh=mesh,
        in_specs=placed,
        out_specs=P(None, ("prow", "pcol"), None, None),
        check_vma=False,
    )
```

time: 120 us -> 93.6 us (0.78)
  Pallas kernels: 118 us -> 91.5 us
    pallas_call x1, Pallas kernels: 118 us -> 91.5 us  [shards(): pl.pallas_call(functools.partial(kernel, n_row, n_col, levels, nnz), out_...]
where the time goes in v6:
time: 93.6 us; the launch traced here: 93.3 us
  Pallas kernels  91.5 us (98%)
  local copies, waits for them, and re-layouts  1.72 us (2%)
    pallas_call x1, Pallas kernels, shards(): pl.pallas_call(functools.partial(kernel, n_row, n_col, levels, nnz), out_...  91.5 us

profile of v6, /device:TPU:0, one launch (start us, length us, event | category | flops | bytes accessed | tf_op | source)
XLA Modules:
  0.0 93.3 jit_solution(7169428689686187461)
XLA Ops:
  0.0 91.5 %shard_map.73 = bf16[5,1,128,256]{3,2,1,0:T(8,128)(2,1)} custom-call(bf16[5,1,128,256]{3,2,1,0:T(8,128)(2,1)} %rhs_hbm.1, bf16[5,1,128,128]{3,2,1,0:T(8,128)(2,1)} %linv_hbm.1, bf16[5,1,128,128]{3,2,1,0:T(8,128)(2,1)} %uinv_hbm.1, bf16[4,4,6,128,128]{4,3,2,1,0:T(8,128)(2,1)} %lblk.1, bf16[4,4,6,128,128]{4,3,2,1,0:T(8,128)(2,1)} %ublk.1, s32[4,4,6]{2,1,0:T(4,128)} %lidx.1, ...), custom_call_target="tpu_custom_call" | custom-call | flops 1610612736 | bytes 6291456 | tf_op jit(solution)/shard_map/pallas_call | solution.py:222
  91.6 1.7 %copy.9 = bf16[5,1,128,256]{3,2,1,0:T(8,128)(2,1)} copy(bf16[5,1,128,256]{3,2,1,0:T(8,128)(2,1)} %shard_map.73) | data formatting | bytes 655360
